TPU v7x, 32 devices: a whole 2x2x4 slice. The times are simulated.
32 devices in a mesh: groups: 2 (over y), space: 8 (over z, x), heads: 2 (over core).
Axes of the slice: x: 2, y: 2, z: 4, core: 2. Of those that a mesh axis runs over, the one named last changes fastest.
Arguments:
- queries: bfloat16 [2400, 1536], P(('groups', 'space'), 'heads'), parts along dimension 0, may hold values from -16 to 16
- latent_keys: bfloat16 [2400, 1536], P(('groups', 'space'), 'heads'), parts along dimension 0, may hold values from -9 to 9
- latent_values: bfloat16 [2400, 1536], P(('groups', 'space'), 'heads'), parts along dimension 0, may hold values from -6 to 6
- prompt: bfloat16 [512, 3072], P('groups'), parts along dimension 0, may hold values from -44 to 44
- key_weight: bfloat16 [3072, 1536], P('space', 'heads'), may hold values from -0.15625 to 0.15625
- value_weight: bfloat16 [3072, 1536], P('space', 'heads'), may hold values from -0.15625 to 0.15625
- out_weight: bfloat16 [1536, 3072], P('heads', 'space'), may hold values from -0.21875 to 0.21875
- tile_owner: int32 [16], P('groups'), parts along dimension 0, may hold values from 0 to 7, as said below
Outputs:
- block_output: bfloat16 [2400, 3072], P(('groups', 'space'), 'heads'), parts along dimension 0
There are 2 independent parts, one for each index of `groups`. A program takes and returns all parts, laid end to end along the dimension named above; an argument that names none is the same for every part. Nothing has to cross between parts.
Inputs may be any that keep to these rules, and one draw needn't show every extreme that they name: `tile_owner`: tile t = i * 2 + j of the 4 x 2 grid is held by slot a * 2 + b, with a = (i + r) mod 4 or a = (3 - i + r) mod 4 for one r, and b = j or b = 1 - j; r and each of the two alternatives are the same for all tiles.
All inputs are finite; a program needn't handle non-finite values.
Results may differ from a plain program's by a relative error of at most 0.0081.
Values may be sent and summed in bfloat16 or wider, within the bound.
A program may use at most 64 MiB of HBM per device.

v0:
```python
import jax
import jax.numpy as jnp
from jax import lax
from jax.sharding import PartitionSpec as P

HD = 128
RT = 16
RH = 56
TILE = 5
rope_theta = 256.0
eps_norm = 1e-06
masked_score = -1e30


def shifted(value, axis, steps):
    count = lax.axis_size(axis)
    pairs = [(source, (source + steps) % count) for source in range(count)]
    return lax.ppermute(value, axis, pairs)


def rope_tables(frame_pos, height_pos, width_pos):
    pairs_time = jnp.arange(RT // 2, dtype=jnp.float32)
    pairs_space = jnp.arange(RH // 2, dtype=jnp.float32)
    freq_time = rope_theta ** (-2.0 * pairs_time / RT)
    freq_space = rope_theta ** (-2.0 * pairs_space / RH)
    angles = jnp.concatenate(
        [
            frame_pos[:, None] * freq_time[None, :],
            height_pos[:, None] * freq_space[None, :],
            width_pos[:, None] * freq_space[None, :],
        ],
        axis=1,
    )
    return (jnp.cos(angles), jnp.sin(angles))


def rotate(stacked, cosine, sine_table):
    row_count = stacked.shape[0]
    head_total = stacked.shape[1]
    paired = stacked.reshape(row_count, head_total, HD // 2, 2)
    even_part = paired[..., 0]
    odd_part = paired[..., 1]
    cos_rows = cosine[:, None, :]
    sin_rows = sine_table[:, None, :]
    turned = jnp.stack(
        [even_part * cos_rows - odd_part * sin_rows, even_part * sin_rows + odd_part * cos_rows],
        axis=-1,
    )
    return turned.reshape(row_count, head_total * HD)


def normalize_keys(summed, head_total):
    row_count = summed.shape[0]
    half_width = summed.shape[1] // 2
    key_part = summed[:, :half_width].reshape(row_count, head_total, HD)
    key_part = key_part * lax.rsqrt(
        jnp.mean(key_part * key_part, axis=-1, keepdims=True) + eps_norm
    )
    return jnp.concatenate(
        [key_part.reshape(row_count, half_width), summed[:, half_width:]], axis=1
    ).astype(jnp.bfloat16)


def body(
    queries, latent_keys, latent_values, prompt, key_weight, value_weight, out_weight, tile_owner
):
    spaces = lax.axis_size("space")
    device = lax.axis_index("space")
    grid_h = min(8, spaces // 2)
    grid_w = spaces // grid_h
    tok_rows = queries.shape[0]
    head_width = queries.shape[1]
    head_count = head_width // HD
    tile_total = tile_owner.shape[0]
    tile_index = jnp.arange(tile_total, dtype=jnp.int32)
    own_tile = jnp.sum(jnp.where(tile_owner == device, tile_index, 0))
    tile_row = own_tile // grid_w
    tile_col = own_tile % grid_w
    anchor_slot = tile_owner[0]
    right_slot = tile_owner[min(1, tile_total - 1)]
    lower_slot = tile_owner[min(grid_w, tile_total - 1)]
    col_sign = jnp.where(right_slot % grid_w - anchor_slot % grid_w == -1, -1, 1)
    row_sign = jnp.where((lower_slot // grid_w - anchor_slot // grid_w) % grid_h == 1, 1, -1)
    cell_index = jnp.arange(tok_rows, dtype=jnp.int32)
    frame_pos = (cell_index // (TILE * TILE)).astype(jnp.float32)
    height_pos = (tile_row * TILE + cell_index // TILE % TILE).astype(jnp.float32)
    width_pos = (tile_col * TILE + cell_index % TILE).astype(jnp.float32)
    cosine, sine_table = rope_tables(frame_pos, height_pos, width_pos)
    query_rot = rotate(
        queries.astype(jnp.float32).reshape(tok_rows, head_count, HD), cosine, sine_table
    ).astype(jnp.bfloat16)
    key_rot = rotate(
        latent_keys.astype(jnp.float32).reshape(tok_rows, head_count, HD), cosine, sine_table
    ).astype(jnp.bfloat16)
    width_rows = key_weight.shape[0]
    text_cols = lax.dynamic_slice_in_dim(prompt, device * width_rows, width_rows, 1)
    both_weights = jnp.concatenate([key_weight, value_weight], axis=1)
    partial_text = jnp.dot(text_cols, both_weights, preferred_element_type=jnp.float32)
    summed_text = lax.psum(partial_text, "space")
    text_kv = normalize_keys(summed_text, head_count)
    kv_own = jnp.concatenate([key_rot, latent_values], axis=1)
    blocks = []
    valid_parts = []
    for row_step in (-1, 0, 1):
        for col_step in (-1, 0, 1):
            if row_step == 0 and col_step == 0:
                fetched = kv_own
            else:
                fetched = shifted(kv_own, "space", -(row_step * grid_w + col_step))
            near_row = tile_row + row_sign * row_step
            near_col = tile_col + col_sign * col_step
            inside = (near_row >= 0) & (near_row < grid_h) & (near_col >= 0) & (near_col < grid_w)
            blocks.append(fetched)
            valid_parts.append(jnp.zeros((tok_rows,), jnp.int32) + inside.astype(jnp.int32))
    blocks.append(text_kv)
    valid_parts.append(jnp.ones((text_kv.shape[0],), jnp.int32))
    keys_all = jnp.concatenate(blocks, axis=0)
    key_valid = jnp.concatenate(valid_parts, axis=0)
    score_scale = HD ** (-0.5)
    head_outputs = []
    for head_index in range(head_count):
        head_start = head_index * HD
        query_slice = query_rot[:, head_start : head_start + HD]
        key_slice = keys_all[:, head_start : head_start + HD]
        value_slice = keys_all[:, head_width + head_start : head_width + head_start + HD]
        scores = (
            lax.dot_general(
                query_slice, key_slice, (((1,), (1,)), ((), ())), preferred_element_type=jnp.float32
            )
            * score_scale
        )
        scores = jnp.where(key_valid[None, :] > 0, scores, masked_score)
        top_score = jnp.max(scores, axis=-1, keepdims=True)
        exponent = jnp.exp(scores - top_score)
        weights = (exponent / jnp.sum(exponent, axis=-1, keepdims=True)).astype(jnp.bfloat16)
        head_outputs.append(
            jnp.dot(weights, value_slice, preferred_element_type=jnp.float32).astype(jnp.bfloat16)
        )
    attended = jnp.concatenate(head_outputs, axis=1)
    partial_out = jnp.dot(
        attended,
        lax.all_gather(out_weight, "space", axis=1, tiled=True),
        preferred_element_type=jnp.float32,
    )
    summed_out = lax.psum_scatter(
        partial_out.astype(jnp.bfloat16), "heads", scatter_dimension=1, tiled=True
    )
    return summed_out


def solution(mesh):
    in_specs = (
        P(("groups", "space"), "heads"),
        P(("groups", "space"), "heads"),
        P(("groups", "space"), "heads"),
        P("groups", None),
        P("space", "heads"),
        P("space", "heads"),
        P("heads", "space"),
        P("groups"),
    )
    out_specs = P(("groups", "space"), "heads")
    return jax.shard_map(body, mesh=mesh, in_specs=in_specs, out_specs=out_specs, check_vma=False)
```

profile of v0, /device:TPU:0, one launch (start us, length us, event | category | flops | bytes accessed | tf_op | source)
XLA Modules:
  0.0 252.2 jit_solution(18399292161967376809)
XLA Ops:
  6.6 1.4 copy-done
  7.9 3.0 %fusion.6 = f32[256,1536]{1,0:T(8,128)} fusion(bf16[384,768]{1,0:T(8,128)(2,1)} %param.13, bf16[384,768]{1,0:T(8,128)(2,1)} %param.12, bf16[256,3072]{1,0:T(8,128)(2,1)S(1)} %copy-done, s32[]{:T(128)S(6)} %select_n.110), kind=kOutput, calls=%fused_computation.13 | convolution fusion | flops 304349184 | bytes 2949124 | tf_op jit(solution)/shard_map/dot_general | solution.py:98
  11.0 0.7 all-gather.2.cloned.1.call-update
  11.7 0.6 fusion.51
  15.2 0.5 reshape.201
  15.7 2.0 copy.10
  17.7 1.6 reshape.202
  19.7 2.7 %subtract_convert_fusion.1 = (bf16[150,6,64,1]{0,3,2,1:T(2,128)(2,1)S(1)}, bf16[150,6,64,1]{0,3,2,1:T(2,128)(2,1)}, bf16[150,6,64,1]{0,3,2,1:T(2,128)(2,1)S(1)}, bf16[150,6,64,1]{0,3,2,1:T(2,128)(2,1)S(1)}) fusion(f32[150,6,64,2]{0,3,2,1:T(2,128)S(1)} %reshape.201, f32[150,64]{0,1:T(8,128)S(1)} %get-tuple-element.12, f32[150,64]{0,1:T(8,128)S(1)} %get-tuple-element.11, ...), kind=kLoop, calls=%fused_computation.69 | loop fusion | flops 921600 | bytes 1459200 | tf_op jit(solution)/shard_map/convert.7
  22.5 1.0 pad_maximum_fusion.3
  23.4 0.4 convert_element_type.111
  24.0 1.7 pad_maximum_fusion.1
  25.7 4.0 %collective-permute-start = (bf16[150,1536]{1,0:T(8,128)(2,1)}, bf16[150,1536]{1,0:T(8,128)(2,1)}, u32[]{:S(2)}, u32[]{:S(2)}) collective-permute-start(bf16[150,1536]{1,0:T(8,128)(2,1)} %pad_maximum_fusion.1), channel_id=1, source_target_pairs={{0,6},{2,8},{4,10},{6,12},{8,14},{10,0},{12,2},{14,4},{1,7},{3,9},... | collective-permute-start | bytes 1382408 | tf_op jit(solution)/shard_map/ppermute | solution.py:18
  29.7 1.6 collective-permute-start.1
  31.3 1.5 collective-permute-start.2
  32.8 3.2 %collective-permute-start.3 = (bf16[150,1536]{1,0:T(8,128)(2,1)}, bf16[150,1536]{1,0:T(8,128)(2,1)}, u32[]{:S(2)}, u32[]{:S(2)}) collective-permute-start(bf16[150,1536]{1,0:T(8,128)(2,1)} %pad_maximum_fusion.1), channel_id=1, source_target_pairs={{0,14},{2,0},{4,2},{6,4},{8,6},{10,8},{12,10},{14,12},{1,15},{3,1}... | collective-permute-start | bytes 1382408 | tf_op jit(solution)/shard_map/ppermute | solution.py:18
  36.0 0.5 collective-permute-start.4
  36.5 0.6 fusion.54
  43.3 2.0 pad_maximum_fusion.2
  45.3 1.1 convert_element_type.110
  46.6 91.5 %all-reduce.2.cloned.1.call-done = f32[256,1536]{1,0:T(8,128)} async-done(((f32[256,1536]{1,0:T(8,128)}), f32[256,1536]{1,0:T(8,128)}) %all-reduce.2.cloned.1.call-update) | async-done | bytes 1572880 | tf_op jit(solution)/shard_map/psum | solution.py:99
  138.1 1.2 slice_multiply_fusion
  139.3 0.3 copy.12
  140.0 1.2 slice.180
  141.2 3.0 %collective-permute-start.5 = (bf16[150,1536]{1,0:T(8,128)(2,1)}, bf16[150,1536]{1,0:T(8,128)(2,1)S(1)}, u32[]{:S(2)}, u32[]{:S(2)}) collective-permute-start(bf16[150,1536]{1,0:T(8,128)(2,1)} %pad_maximum_fusion.1), channel_id=1, source_target_pairs={{0,10},{2,12},{4,14},{6,0},{8,2},{10,4},{12,6},{14,8},{1,11},{3,13... | collective-permute-start | bytes 1382408 | tf_op jit(solution)/shard_map/ppermute | solution.py:18
  144.1 1.2 multiply_convert_fusion
  145.4 16.0 %collective-permute-done.5 = bf16[150,1536]{1,0:T(8,128)(2,1)S(1)} collective-permute-done((bf16[150,1536]{1,0:T(8,128)(2,1)}, bf16[150,1536]{1,0:T(8,128)(2,1)S(1)}, u32[]{:S(2)}, u32[]{:S(2)}) %collective-permute-start.5) | collective-permute-done | bytes 460832 | tf_op jit(solution)/shard_map/ppermute | solution.py:18
  161.5 34.4 %concatenate.39 = bf16[1606,1536]{1,0:T(8,128)(2,1)} concatenate(bf16[150,1536]{1,0:T(8,128)(2,1)} %collective-permute-done, bf16[150,1536]{1,0:T(8,128)(2,1)} %collective-permute-done.1, bf16[150,1536]{1,0:T(8,128)(2,1)} %collective-permute-done.2, bf16[150,1536]{1,0:T(8,128)(2,1)} %collective-permute-done.2, bf16[150,1536]{1,0:T(8,128)(2,1)} %pad_maximum_fusion.1, ...), dimensions={0} | concatenate | bytes 9867264 | tf_op jit(solution)/shard_map/concatenate | solution.py:117
  195.9 1.6 fusion.55
  197.5 0.3 fusion.16
  197.8 1.6 fusion.56
  199.4 0.3 fusion.17
  199.7 1.7 fusion.57
  201.4 0.3 fusion.18
  201.7 1.6 fusion.58
  203.3 0.3 fusion.19
  203.5 1.6 fusion.59
  205.1 0.3 fusion.20
  205.4 1.6 fusion.60
  207.0 0.3 fusion.21
  207.3 0.4 fusion.15
  207.7 0.4 fusion.14
  208.2 0.4 fusion.13
  208.6 0.4 fusion.12
  209.0 0.4 fusion.11
  209.4 0.4 fusion.10
  209.9 22.8 %all-gather.2.cloned.1.call-done = bf16[768,3072]{1,0:T(8,128)(2,1)} async-done(((bf16[768,384]{1,0:T(8,128)(2,1)}), bf16[768,3072]{1,0:T(8,128)(2,1)}) %all-gather.2.cloned.1.call-update) | async-done | bytes 4718608 | tf_op jit(solution)/shard_map/all_gather | solution.py:142
  232.6 4.2 %convolution_convert_fusion = bf16[150,3072]{1,0:T(8,128)(2,1)} fusion(bf16[150,768]{1,0:T(8,128)(2,1)S(1)} %fusion.10, bf16[768,3072]{1,0:T(8,128)(2,1)} %all-gather.2.cloned.1.call-done), kind=kOutput, calls=%fused_computation | convolution fusion | flops 708249600 | bytes 5870592 | tf_op jit(solution)/shard_map/dot_general | solution.py:140
  236.8 8.8 %reduce-scatter.2.cloned.1.call-done = bf16[150,1536]{1,0:T(8,128)(2,1)} async-done(((bf16[150,3072]{1,0:T(8,128)(2,1)}), bf16[150,1536]{1,0:T(8,128)(2,1)}) %reduce-scatter.2.cloned.1.call-update) | async-done | bytes 460816 | tf_op jit(solution)/shard_map/reduce_scatter | solution.py:145
  (43 shorter events, 1.5 us)
Async XLA Ops:
  6.5 1.4 copy-start
  6.5 5.2 %copy-start.3 = (s32[8]{0:T(128)S(1)}, s32[8]{0:T(128)}, u32[]{:S(2)}) copy-start(s32[8]{0:T(128)} %param.15) | copy-start | bytes 100
  6.5 8.4 %copy-start.2 = (bf16[150,768]{1,0:T(8,128)(2,1)S(1)}, bf16[150,768]{1,0:T(8,128)(2,1)}, u32[]{:S(2)}) copy-start(bf16[150,768]{1,0:T(8,128)(2,1)} %param.8) | copy-start | bytes 691204
  6.5 131.5 %all-reduce.2.cloned.1.call-start = ((), (), s32[]{:S(2)}) async-start(), calls=%async_computation.1 | async-start | bytes 3145728 | tf_op jit(solution)/shard_map/psum | solution.py:99
  10.9 221.7 %all-gather.2.cloned.1.call-start = ((), (), s32[]{:S(2)}) async-start(), calls=%async_computation.2 | async-start | bytes 5308416 | tf_op jit(solution)/shard_map/all_gather | solution.py:142
  11.7 234.0 %reduce-scatter.2.cloned.1.call-start = ((), (), s32[]{:S(2)}) async-start(), calls=%async_computation.3 | async-start | bytes 1400832 | tf_op jit(solution)/shard_map/reduce_scatter | solution.py:145
  25.7 115.4 %collective-permute-start = (bf16[150,1536]{1,0:T(8,128)(2,1)}, bf16[150,1536]{1,0:T(8,128)(2,1)}, u32[]{:S(2)}, u32[]{:S(2)}) collective-permute-start(bf16[150,1536]{1,0:T(8,128)(2,1)} %pad_maximum_fusion.1), channel_id=1, source_target_pairs={{0,6},{2,8},{4,10},{6,12},{8,14},{10,0},{12,2},{14,4},{1,7},{3,9},... | collective-permute-start | bytes 1382408 | tf_op jit(solution)/shard_map/ppermute | solution.py:18
  29.7 115.7 %collective-permute-start.1 = (bf16[150,1536]{1,0:T(8,128)(2,1)}, bf16[150,1536]{1,0:T(8,128)(2,1)}, u32[]{:S(2)}, u32[]{:S(2)}) collective-permute-start(bf16[150,1536]{1,0:T(8,128)(2,1)} %pad_maximum_fusion.1), channel_id=1, source_target_pairs={{0,4},{2,6},{4,8},{6,10},{8,12},{10,14},{12,0},{14,2},{1,5},{3,7},... | collective-permute-start | bytes 1382408 | tf_op jit(solution)/shard_map/ppermute | solution.py:18
  31.3 114.1 %collective-permute-start.2 = (bf16[150,1536]{1,0:T(8,128)(2,1)}, bf16[150,1536]{1,0:T(8,128)(2,1)}, u32[]{:S(2)}, u32[]{:S(2)}) collective-permute-start(bf16[150,1536]{1,0:T(8,128)(2,1)} %pad_maximum_fusion.1), channel_id=1, source_target_pairs={{0,2},{2,4},{4,6},{6,8},{8,10},{10,12},{12,14},{14,0},{1,3},{3,5},... | collective-permute-start | bytes 1382408 | tf_op jit(solution)/shard_map/ppermute | solution.py:18
  32.8 112.6 %collective-permute-start.3 = (bf16[150,1536]{1,0:T(8,128)(2,1)}, bf16[150,1536]{1,0:T(8,128)(2,1)}, u32[]{:S(2)}, u32[]{:S(2)}) collective-permute-start(bf16[150,1536]{1,0:T(8,128)(2,1)} %pad_maximum_fusion.1), channel_id=1, source_target_pairs={{0,14},{2,0},{4,2},{6,4},{8,6},{10,8},{12,10},{14,12},{1,15},{3,1}... | collective-permute-start | bytes 1382408 | tf_op jit(solution)/shard_map/ppermute | solution.py:18
  36.0 109.4 %collective-permute-start.4 = (bf16[150,1536]{1,0:T(8,128)(2,1)}, bf16[150,1536]{1,0:T(8,128)(2,1)}, u32[]{:S(2)}, u32[]{:S(2)}) collective-permute-start(bf16[150,1536]{1,0:T(8,128)(2,1)} %pad_maximum_fusion.1), channel_id=1, source_target_pairs={{0,12},{2,14},{4,0},{6,2},{8,4},{10,6},{12,8},{14,10},{1,13},{3,15... | collective-permute-start | bytes 1382408 | tf_op jit(solution)/shard_map/ppermute | solution.py:18
  141.2 20.3 %collective-permute-start.5 = (bf16[150,1536]{1,0:T(8,128)(2,1)}, bf16[150,1536]{1,0:T(8,128)(2,1)S(1)}, u32[]{:S(2)}, u32[]{:S(2)}) collective-permute-start(bf16[150,1536]{1,0:T(8,128)(2,1)} %pad_maximum_fusion.1), channel_id=1, source_target_pairs={{0,10},{2,12},{4,14},{6,0},{8,2},{10,4},{12,6},{14,8},{1,11},{3,13... | collective-permute-start | bytes 1382408 | tf_op jit(solution)/shard_map/ppermute | solution.py:18
  199.6 7.7 %copy-start.1 = (bf16[1606,1536]{1,0:T(8,128)(2,1)S(1)}, bf16[1606,1536]{1,0:T(8,128)(2,1)}, u32[]{:S(2)}) copy-start(bf16[1606,1536]{1,0:T(8,128)(2,1)} %concatenate.39) | copy-start | bytes 14800900
Sparse Core Ops, SparseCore 0:
  11.1 126.9 all-reduce.1
  140.1 92.4 all-gather.1
  237.0 8.6 reduce-scatter.1
where the time goes:
time: 254 us; the launch traced here: 252 us
  waiting for transfers between devices  140 us (55%)
  local copies, waits for them, and re-layouts  44.1 us (17%)
  between operations  22.3 us (9%)
  matrix products  19.3 us (8%)
  starting transfers between devices  13.8 us (5%)
  other arithmetic  12.8 us (5%)
    psum x1, waiting for transfers between devices, body(): summed_text = lax.psum(partial_text, 'space')  91.5 us
    concatenate x1, local copies, waits for them, and re-layouts, body(): keys_all = jnp.concatenate(blocks, axis=0)  34.4 us
    all_gather x1, waiting for transfers between devices, body(): lax.all_gather(out_weight, 'space', axis=1, tiled=True)  22.8 us
    ppermute x6, waiting for transfers between devices, shifted(): return lax.ppermute(value, axis, pairs)  16.1 us
    ppermute x6, starting transfers between devices, shifted(): return lax.ppermute(value, axis, pairs)  13.7 us
    dot_general x6, matrix products, body(): lax.dot_general(query_slice, key_slice, (((1,), (1,)), ((), ())), preferr...  9.63 us
    reduce_scatter x1, waiting for transfers between devices, body(): lax.psum_scatter(partial_out.astype(jnp.bfloat16), 'heads', scatter_dimen...  8.8 us
  transfers between devices with their start and end apart: 9, of which 4 were waited for; matrix products, arithmetic and copies ran while one was open for 27% of the time, Pallas kernels for 0%

commit v1 on v0

--- a/solution.py
+++ b/solution.py
@@ -1,7 +1,9 @@
+import functools
 import jax
 import jax.numpy as jnp
 from jax import lax
 from jax.sharding import PartitionSpec as P
+from jax.lax import axis_index, ppermute, psum
 
 HD = 128
 RT = 16
@@ -10,6 +12,33 @@
 rope_theta = 256.0
 eps_norm = 1e-06
 masked_score = -1e30
+
+
+def _connect_slots(raw, axis_id, d_out):
+    value_now, o_now, step_out = (psum(1, axis_id), axis_index(axis_id), raw.shape[d_out])
+    wide_out = lax.dynamic_update_slice_in_dim(
+        jnp.zeros([t * value_now if c == d_out else t for c, t in enumerate(raw.shape)], raw.dtype),
+        raw,
+        o_now * step_out,
+        axis=d_out,
+    )
+    big = local_next = raw
+    for k0 in range(1, value_now // 2 + 1):
+        big = ppermute(big, axis_id, [(c, (c + 1) % value_now) for c in range(value_now)])
+        wide_out = lax.dynamic_update_slice_in_dim(
+            wide_out, big, (o_now - k0) % value_now * step_out, axis=d_out
+        )
+        if 2 * k0 < value_now:
+            local_next = ppermute(
+                local_next, axis_id, [(c, (c - 1) % value_now) for c in range(value_now)]
+            )
+            wide_out = lax.dynamic_update_slice_in_dim(
+                wide_out, local_next, (o_now + k0) % value_now * step_out, axis=d_out
+            )
+    return wide_out
+
+
+extend_units = functools.partial(_connect_slots, axis_id="space", d_out=1)
 
 
 def shifted(value, axis, steps):
@@ -137,11 +166,7 @@
             jnp.dot(weights, value_slice, preferred_element_type=jnp.float32).astype(jnp.bfloat16)
         )
     attended = jnp.concatenate(head_outputs, axis=1)
-    partial_out = jnp.dot(
-        attended,
-        lax.all_gather(out_weight, "space", axis=1, tiled=True),
-        preferred_element_type=jnp.float32,
-    )
+    partial_out = jnp.dot(attended, extend_units(out_weight), preferred_element_type=jnp.float32)
     summed_out = lax.psum_scatter(
         partial_out.astype(jnp.bfloat16), "heads", scatter_dimension=1, tiled=True
     )

time: 254 us -> 287 us (1.13)
  starting transfers between devices: 13.8 us -> 41.8 us
  local copies, waits for them, and re-layouts: 44.1 us -> 58.2 us
  waiting for transfers between devices: 140 us -> 132 us
    ppermute x0 -> x7, waiting for transfers between devices: none -> 64.7 us  [the longest x4 50.4 us: _connect_slots(): ppermute(big, axis_id, [(c, (c + 1) % value_now) for c in range(value_now)])]
    psum x1, waiting for transfers between devices: 91.5 us -> 54.7 us  [body(): summed_text = lax.psum(partial_text, 'space')]
    ppermute x0 -> x7, starting transfers between devices: none -> 29.9 us  [the longest x4 19.1 us: _connect_slots(): ppermute(big, axis_id, [(c, (c + 1) % value_now) for c in range(value_now)])]
    all_gather x1 -> x0, waiting for transfers between devices: 22.8 us -> none  [body(): lax.all_gather(out_weight, 'space', axis=1, tiled=True)]
    dynamic_update_slice x0 -> x8, local copies, waits for them, and re-layouts: none -> 10.9 us  [the longest x3 5.03 us: _connect_slots(): lax.dynamic_update_slice_in_dim(wide_out, local_next, (o_now + k0) % valu...]
    ppermute x6, waiting for transfers between devices: 16.1 us -> 5.42 us  [shifted(): return lax.ppermute(value, axis, pairs)]
  transfers between devices with their start and end apart: 9 -> 15, of which waited for: 4 -> 7; matrix products, arithmetic and copies ran while one was open for 27% -> 29% of each run, Pallas kernels for 0% -> 0%
where the time goes in v1:
time: 287 us; the launch traced here: 285 us
  waiting for transfers between devices  132 us (46%)
  local copies, waits for them, and re-layouts  58.2 us (20%)
  starting transfers between devices  41.8 us (15%)
  between operations  22.8 us (8%)
  matrix products  17.1 us (6%)
  other arithmetic  13.4 us (5%)
    psum x1, waiting for transfers between devices, body(): summed_text = lax.psum(partial_text, 'space')  54.7 us
    ppermute x4, waiting for transfers between devices, _connect_slots(): ppermute(big, axis_id, [(c, (c + 1) % value_now) for c in range(value_now)])  50.4 us
    concatenate x1, local copies, waits for them, and re-layouts, body(): keys_all = jnp.concatenate(blocks, axis=0)  36.1 us
    ppermute x4, starting transfers between devices, _connect_slots(): ppermute(big, axis_id, [(c, (c + 1) % value_now) for c in range(value_now)])  19.1 us
    ppermute x3, waiting for transfers between devices, _connect_slots(): ppermute(local_next, axis_id, [(c, (c - 1) % value_now) for c in range(va...  14.3 us
    ppermute x6, starting transfers between devices, shifted(): return lax.ppermute(value, axis, pairs)  11.8 us
    ppermute x3, starting transfers between devices, _connect_slots(): ppermute(local_next, axis_id, [(c, (c - 1) % value_now) for c in range(va...  10.8 us
    dot_general x6, matrix products, body(): lax.dot_general(query_slice, key_slice, (((1,), (1,)), ((), ())), preferr...  7.38 us
  transfers between devices with their start and end apart: 15, of which 7 were waited for; matrix products, arithmetic and copies ran while one was open for 29% of the time, Pallas kernels for 0%

profile of v1, /device:TPU:0, one launch (start us, length us, event | category | flops | bytes accessed | tf_op | source)
XLA Modules:
  0.0 285.3 jit_solution(8143537618062802308)
XLA Ops:
  6.5 2.9 %collective-permute-start.6 = (bf16[768,384]{1,0:T(8,128)(2,1)}, bf16[768,384]{1,0:T(8,128)(2,1)}, u32[]{:S(2)}, u32[]{:S(2)}) collective-permute-start(bf16[768,384]{1,0:T(8,128)(2,1)} %param.14), channel_id=1, source_target_pairs={{0,2},{2,4},{4,6},{6,8},{8,10},{10,12},{12,14},{14,0},{1,3},{3,5},... | collective-permute-start | bytes 1769480 | tf_op jit(solution)/shard_map/ppermute | solution.py:27
  9.5 3.1 %collective-permute-start.7 = (bf16[768,384]{1,0:T(8,128)(2,1)}, bf16[768,384]{1,0:T(8,128)(2,1)}, u32[]{:S(2)}, u32[]{:S(2)}) collective-permute-start(bf16[768,384]{1,0:T(8,128)(2,1)} %param.14), channel_id=1, source_target_pairs={{0,14},{2,0},{4,2},{6,4},{8,6},{10,8},{12,10},{14,12},{1,15},{3,1}... | collective-permute-start | bytes 1769480 | tf_op jit(solution)/shard_map/ppermute | solution.py:32
  12.6 3.0 %fusion.6 = f32[256,1536]{1,0:T(8,128)} fusion(bf16[384,768]{1,0:T(8,128)(2,1)} %param.13, bf16[384,768]{1,0:T(8,128)(2,1)} %param.12, bf16[256,3072]{1,0:T(8,128)(2,1)S(1)} %copy-done, s32[]{:T(128)S(6)} %select_n.160), kind=kOutput, calls=%fused_computation.13 | convolution fusion | flops 304349184 | bytes 2949124 | tf_op jit(solution)/shard_map/dot_general | solution.py:127
  15.6 1.3 fusion.52
  20.3 2.0 copy.10
  22.3 1.6 reshape.202
  24.3 2.7 subtract_convert_fusion.1
  27.0 1.0 pad_maximum_fusion.3
  28.5 1.7 pad_maximum_fusion.1
  30.3 1.5 collective-permute-start.1
  31.8 2.4 collective-permute-start.2
  34.2 0.6 fusion.54
  41.2 2.0 pad_maximum_fusion.2
  43.9 6.9 %collective-permute-done.6 = bf16[768,384]{1,0:T(8,128)(2,1)} collective-permute-done((bf16[768,384]{1,0:T(8,128)(2,1)}, bf16[768,384]{1,0:T(8,128)(2,1)}, u32[]{:S(2)}, u32[]{:S(2)}) %collective-permute-start.6) | collective-permute-done | bytes 589856 | tf_op jit(solution)/shard_map/ppermute | solution.py:27
  50.8 2.9 %collective-permute-start.8 = (bf16[768,384]{1,0:T(8,128)(2,1)}, bf16[768,384]{1,0:T(8,128)(2,1)S(1)}, u32[]{:S(2)}, u32[]{:S(2)}) collective-permute-start(bf16[768,384]{1,0:T(8,128)(2,1)} %collective-permute-done.6), channel_id=1, source_target_pairs={{0,2},{2,4},{4,6},{6,8},{8,10},{10,12},{12,14},{14,0},{1,3},{3,5},... | collective-permute-start | bytes 1769480 | tf_op jit(solution)/shard_map/ppermute | solution.py:27
  53.7 2.8 broadcast_in_dim.75
  56.4 1.0 constant_dynamic-update-slice_fusion.7
  57.4 3.6 %collective-permute-start.9 = (bf16[768,384]{1,0:T(8,128)(2,1)}, bf16[768,384]{1,0:T(8,128)(2,1)S(1)}, u32[]{:S(2)}, u32[]{:S(2)}) collective-permute-start(bf16[768,384]{1,0:T(8,128)(2,1)} %collective-permute-done.7), channel_id=1, source_target_pairs={{0,14},{2,0},{4,2},{6,4},{8,6},{10,8},{12,10},{14,12},{1,15},{3,1}... | collective-permute-start | bytes 1769480 | tf_op jit(solution)/shard_map/ppermute | solution.py:32
  61.0 2.0 constant_dynamic-update-slice_fusion.6
  63.0 2.1 constant_dynamic-update-slice_fusion.5
  65.0 21.2 %collective-permute-done.8 = bf16[768,384]{1,0:T(8,128)(2,1)S(1)} collective-permute-done((bf16[768,384]{1,0:T(8,128)(2,1)}, bf16[768,384]{1,0:T(8,128)(2,1)S(1)}, u32[]{:S(2)}, u32[]{:S(2)}) %collective-permute-start.8) | collective-permute-done | bytes 589856 | tf_op jit(solution)/shard_map/ppermute | solution.py:27
  86.3 5.1 %collective-permute-start.3 = (bf16[150,1536]{1,0:T(8,128)(2,1)}, bf16[150,1536]{1,0:T(8,128)(2,1)}, u32[]{:S(2)}, u32[]{:S(2)}) collective-permute-start(bf16[150,1536]{1,0:T(8,128)(2,1)} %pad_maximum_fusion.1), channel_id=1, source_target_pairs={{0,14},{2,0},{4,2},{6,4},{8,6},{10,8},{12,10},{14,12},{1,15},{3,1}... | collective-permute-start | bytes 1382408 | tf_op jit(solution)/shard_map/ppermute | solution.py:47
  91.3 1.0 constant_dynamic-update-slice_fusion.4
  92.4 14.3 %collective-permute-done.9 = bf16[768,384]{1,0:T(8,128)(2,1)S(1)} collective-permute-done((bf16[768,384]{1,0:T(8,128)(2,1)}, bf16[768,384]{1,0:T(8,128)(2,1)S(1)}, u32[]{:S(2)}, u32[]{:S(2)}) %collective-permute-start.9) | collective-permute-done | bytes 589856 | tf_op jit(solution)/shard_map/ppermute | solution.py:32
  106.6 0.8 copy-done.3
  107.5 0.9 constant_dynamic-update-slice_fusion.3
  108.4 54.7 %all-reduce.2.cloned.1.call-done = f32[256,1536]{1,0:T(8,128)} async-done(((f32[256,1536]{1,0:T(8,128)}), f32[256,1536]{1,0:T(8,128)}) %all-reduce.2.cloned.1.call-update) | async-done | bytes 1572880 | tf_op jit(solution)/shard_map/psum | solution.py:128
  163.1 1.2 slice_multiply_fusion
  165.0 1.2 slice.180
  166.2 2.8 collective-permute-start.5
  168.9 1.2 multiply_convert_fusion
  170.2 0.6 collective-permute-start.10
  170.8 4.2 %collective-permute-start.11 = (bf16[768,384]{1,0:T(8,128)(2,1)}, bf16[768,384]{1,0:T(8,128)(2,1)}, u32[]{:S(2)}, u32[]{:S(2)}) collective-permute-start(bf16[768,384]{1,0:T(8,128)(2,1)} %copy-done.3), channel_id=1, source_target_pairs={{0,14},{2,0},{4,2},{6,4},{8,6},{10,8},{12,10},{14,12},{1,15},{3,1}... | collective-permute-start | bytes 1769480 | tf_op jit(solution)/shard_map/ppermute | solution.py:32
  175.0 5.4 %collective-permute-done.5 = bf16[150,1536]{1,0:T(8,128)(2,1)} collective-permute-done((bf16[150,1536]{1,0:T(8,128)(2,1)}, bf16[150,1536]{1,0:T(8,128)(2,1)}, u32[]{:S(2)}, u32[]{:S(2)}) %collective-permute-start.5) | collective-permute-done | bytes 460832 | tf_op jit(solution)/shard_map/ppermute | solution.py:47
  180.4 36.1 %concatenate.39 = bf16[1606,1536]{1,0:T(8,128)(2,1)} concatenate(bf16[150,1536]{1,0:T(8,128)(2,1)} %collective-permute-done, bf16[150,1536]{1,0:T(8,128)(2,1)} %collective-permute-done.1, bf16[150,1536]{1,0:T(8,128)(2,1)} %collective-permute-done.2, bf16[150,1536]{1,0:T(8,128)(2,1)} %collective-permute-done.2, bf16[150,1536]{1,0:T(8,128)(2,1)} %pad_maximum_fusion.1, ...), dimensions={0} | concatenate | bytes 9867264 | tf_op jit(solution)/shard_map/concatenate | solution.py:146
  216.5 1.7 fusion.55
  218.2 1.5 fusion.56
  219.8 1.5 fusion.57
  221.3 1.5 fusion.58
  222.8 0.5 fusion.59
  227.0 0.5 fusion.60
  227.5 12.6 %collective-permute-start.12 = (bf16[768,384]{1,0:T(8,128)(2,1)S(1)}, bf16[768,384]{1,0:T(8,128)(2,1)S(1)}, u32[]{:S(2)}, u32[]{:S(2)}) collective-permute-start(bf16[768,384]{1,0:T(8,128)(2,1)S(1)} %collective-permute-done.10), channel_id=1, source_target_pairs={{0,2},{2,4},{4,6},{6,8},{8,10},{10,12},{12,14},{14,0},{1,3},{3,5},... | collective-permute-start | bytes 1769480 | tf_op jit(solution)/shard_map/ppermute | solution.py:27
  240.9 1.0 constant_dynamic-update-slice_fusion.2
  241.8 2.0 constant_dynamic-update-slice_fusion.1
  243.9 22.3 %collective-permute-done.12 = bf16[768,384]{1,0:T(8,128)(2,1)S(1)} collective-permute-done((bf16[768,384]{1,0:T(8,128)(2,1)S(1)}, bf16[768,384]{1,0:T(8,128)(2,1)S(1)}, u32[]{:S(2)}, u32[]{:S(2)}) %collective-permute-start.12) | collective-permute-done | bytes 589856 | tf_op jit(solution)/shard_map/ppermute | solution.py:27
  266.2 0.9 constant_dynamic-update-slice_fusion
  267.2 4.2 %convolution_convert_fusion = bf16[150,3072]{1,0:T(8,128)(2,1)} fusion(bf16[150,768]{1,0:T(8,128)(2,1)S(1)} %fusion.10, bf16[768,3072]{1,0:T(8,128)(2,1)} %constant_dynamic-update-slice_fusion), kind=kOutput, calls=%fused_computation | convolution fusion | flops 708249600 | bytes 5870592 | tf_op jit(solution)/shard_map/dot_general | solution.py:169
  271.4 7.1 %reduce-scatter.2.cloned.1.call-done = bf16[150,1536]{1,0:T(8,128)(2,1)} async-done(((bf16[150,3072]{1,0:T(8,128)(2,1)}), bf16[150,1536]{1,0:T(8,128)(2,1)}) %reduce-scatter.2.cloned.1.call-update) | async-done | bytes 460816 | tf_op jit(solution)/shard_map/reduce_scatter | solution.py:170
  (69 shorter events, 7.2 us)
Async XLA Ops:
  6.5 6.1 %copy-start = (bf16[256,3072]{1,0:T(8,128)(2,1)S(1)}, bf16[256,3072]{1,0:T(8,128)(2,1)}, u32[]{:S(2)}) copy-start(bf16[256,3072]{1,0:T(8,128)(2,1)} %param.11) | copy-start | bytes 4718596
  6.5 13.0 %copy-start.5 = (bf16[150,768]{1,0:T(8,128)(2,1)S(1)}, bf16[150,768]{1,0:T(8,128)(2,1)}, u32[]{:S(2)}) copy-start(bf16[150,768]{1,0:T(8,128)(2,1)} %param.8) | copy-start | bytes 691204
  6.5 156.6 %all-reduce.2.cloned.1.call-start = ((), (), s32[]{:S(2)}) async-start(), calls=%async_computation.1 | async-start | bytes 3145728 | tf_op jit(solution)/shard_map/psum | solution.py:128
  6.5 44.2 %collective-permute-start.6 = (bf16[768,384]{1,0:T(8,128)(2,1)}, bf16[768,384]{1,0:T(8,128)(2,1)}, u32[]{:S(2)}, u32[]{:S(2)}) collective-permute-start(bf16[768,384]{1,0:T(8,128)(2,1)} %param.14), channel_id=1, source_target_pairs={{0,2},{2,4},{4,6},{6,8},{8,10},{10,12},{12,14},{14,0},{1,3},{3,5},... | collective-permute-start | bytes 1769480 | tf_op jit(solution)/shard_map/ppermute | solution.py:27
  9.5 48.0 %collective-permute-start.7 = (bf16[768,384]{1,0:T(8,128)(2,1)}, bf16[768,384]{1,0:T(8,128)(2,1)}, u32[]{:S(2)}, u32[]{:S(2)}) collective-permute-start(bf16[768,384]{1,0:T(8,128)(2,1)} %param.14), channel_id=1, source_target_pairs={{0,14},{2,0},{4,2},{6,4},{8,6},{10,8},{12,10},{14,12},{1,15},{3,1}... | collective-permute-start | bytes 1769480 | tf_op jit(solution)/shard_map/ppermute | solution.py:32
  15.6 262.8 %reduce-scatter.2.cloned.1.call-start = ((), (), s32[]{:S(2)}) async-start(), calls=%async_computation.2 | async-start | bytes 1400832 | tf_op jit(solution)/shard_map/reduce_scatter | solution.py:170
  20.3 14.0 %copy-start.6 = (s32[8]{0:T(128)S(1)}, s32[8]{0:T(128)}, u32[]{:S(2)}) copy-start(s32[8]{0:T(128)} %param.15) | copy-start | bytes 100
  28.0 28.4 %copy-start.2 = (bf16[768,384]{1,0:T(8,128)(2,1)S(1)}, bf16[768,384]{1,0:T(8,128)(2,1)}, u32[]{:S(2)}) copy-start(bf16[768,384]{1,0:T(8,128)(2,1)} %param.14) | copy-start | bytes 1769476
  30.3 135.9 %collective-permute-start = (bf16[150,1536]{1,0:T(8,128)(2,1)}, bf16[150,1536]{1,0:T(8,128)(2,1)}, u32[]{:S(2)}, u32[]{:S(2)}) collective-permute-start(bf16[150,1536]{1,0:T(8,128)(2,1)} %pad_maximum_fusion.1), channel_id=1, source_target_pairs={{0,6},{2,8},{4,10},{6,12},{8,14},{10,0},{12,2},{14,4},{1,7},{3,9},... | collective-permute-start | bytes 1382408 | tf_op jit(solution)/shard_map/ppermute | solution.py:47
  30.3 139.9 %collective-permute-start.1 = (bf16[150,1536]{1,0:T(8,128)(2,1)}, bf16[150,1536]{1,0:T(8,128)(2,1)}, u32[]{:S(2)}, u32[]{:S(2)}) collective-permute-start(bf16[150,1536]{1,0:T(8,128)(2,1)} %pad_maximum_fusion.1), channel_id=1, source_target_pairs={{0,4},{2,6},{4,8},{6,10},{8,12},{10,14},{12,0},{14,2},{1,5},{3,7},... | collective-permute-start | bytes 1382408 | tf_op jit(solution)/shard_map/ppermute | solution.py:47
  31.8 139.0 %collective-permute-start.2 = (bf16[150,1536]{1,0:T(8,128)(2,1)}, bf16[150,1536]{1,0:T(8,128)(2,1)}, u32[]{:S(2)}, u32[]{:S(2)}) collective-permute-start(bf16[150,1536]{1,0:T(8,128)(2,1)} %pad_maximum_fusion.1), channel_id=1, source_target_pairs={{0,2},{2,4},{4,6},{6,8},{8,10},{10,12},{12,14},{14,0},{1,3},{3,5},... | collective-permute-start | bytes 1382408 | tf_op jit(solution)/shard_map/ppermute | solution.py:47
  50.8 35.5 %collective-permute-start.8 = (bf16[768,384]{1,0:T(8,128)(2,1)}, bf16[768,384]{1,0:T(8,128)(2,1)S(1)}, u32[]{:S(2)}, u32[]{:S(2)}) collective-permute-start(bf16[768,384]{1,0:T(8,128)(2,1)} %collective-permute-done.6), channel_id=1, source_target_pairs={{0,2},{2,4},{4,6},{6,8},{8,10},{10,12},{12,14},{14,0},{1,3},{3,5},... | collective-permute-start | bytes 1769480 | tf_op jit(solution)/shard_map/ppermute | solution.py:27
  57.4 49.2 %collective-permute-start.9 = (bf16[768,384]{1,0:T(8,128)(2,1)}, bf16[768,384]{1,0:T(8,128)(2,1)S(1)}, u32[]{:S(2)}, u32[]{:S(2)}) collective-permute-start(bf16[768,384]{1,0:T(8,128)(2,1)} %collective-permute-done.7), channel_id=1, source_target_pairs={{0,14},{2,0},{4,2},{6,4},{8,6},{10,8},{12,10},{14,12},{1,15},{3,1}... | collective-permute-start | bytes 1769480 | tf_op jit(solution)/shard_map/ppermute | solution.py:32
  86.3 20.4 %copy-start.4 = (bf16[768,384]{1,0:T(8,128)(2,1)}, bf16[768,384]{1,0:T(8,128)(2,1)S(1)}, u32[]{:S(2)}) copy-start(bf16[768,384]{1,0:T(8,128)(2,1)S(1)} %collective-permute-done.8) | copy-start | bytes 1769476
  86.3 88.7 %collective-permute-start.3 = (bf16[150,1536]{1,0:T(8,128)(2,1)}, bf16[150,1536]{1,0:T(8,128)(2,1)}, u32[]{:S(2)}, u32[]{:S(2)}) collective-permute-start(bf16[150,1536]{1,0:T(8,128)(2,1)} %pad_maximum_fusion.1), channel_id=1, source_target_pairs={{0,14},{2,0},{4,2},{6,4},{8,6},{10,8},{12,10},{14,12},{1,15},{3,1}... | collective-permute-start | bytes 1382408 | tf_op jit(solution)/shard_map/ppermute | solution.py:47
  106.6 0.8 copy-start.3
  106.6 68.4 %collective-permute-start.4 = (bf16[150,1536]{1,0:T(8,128)(2,1)}, bf16[150,1536]{1,0:T(8,128)(2,1)}, u32[]{:S(2)}, u32[]{:S(2)}) collective-permute-start(bf16[150,1536]{1,0:T(8,128)(2,1)} %pad_maximum_fusion.1), channel_id=1, source_target_pairs={{0,12},{2,14},{4,0},{6,2},{8,4},{10,6},{12,8},{14,10},{1,13},{3,15... | collective-permute-start | bytes 1382408 | tf_op jit(solution)/shard_map/ppermute | solution.py:47
  166.2 14.2 %collective-permute-start.5 = (bf16[150,1536]{1,0:T(8,128)(2,1)}, bf16[150,1536]{1,0:T(8,128)(2,1)}, u32[]{:S(2)}, u32[]{:S(2)}) collective-permute-start(bf16[150,1536]{1,0:T(8,128)(2,1)} %pad_maximum_fusion.1), channel_id=1, source_target_pairs={{0,10},{2,12},{4,14},{6,0},{8,2},{10,4},{12,6},{14,8},{1,11},{3,13... | collective-permute-start | bytes 1382408 | tf_op jit(solution)/shard_map/ppermute | solution.py:47
  170.2 57.3 %collective-permute-start.10 = (bf16[768,384]{1,0:T(8,128)(2,1)}, bf16[768,384]{1,0:T(8,128)(2,1)S(1)}, u32[]{:S(2)}, u32[]{:S(2)}) collective-permute-start(bf16[768,384]{1,0:T(8,128)(2,1)} %copy-done.4), channel_id=1, source_target_pairs={{0,2},{2,4},{4,6},{6,8},{8,10},{10,12},{12,14},{14,0},{1,3},{3,5},... | collective-permute-start | bytes 1769480 | tf_op jit(solution)/shard_map/ppermute | solution.py:27
  170.8 71.0 %collective-permute-start.11 = (bf16[768,384]{1,0:T(8,128)(2,1)}, bf16[768,384]{1,0:T(8,128)(2,1)}, u32[]{:S(2)}, u32[]{:S(2)}) collective-permute-start(bf16[768,384]{1,0:T(8,128)(2,1)} %copy-done.3), channel_id=1, source_target_pairs={{0,14},{2,0},{4,2},{6,4},{8,6},{10,8},{12,10},{14,12},{1,15},{3,1}... | collective-permute-start | bytes 1769480 | tf_op jit(solution)/shard_map/ppermute | solution.py:32
  216.5 6.3 %copy-start.1 = (bf16[1606,1536]{1,0:T(8,128)(2,1)S(1)}, bf16[1606,1536]{1,0:T(8,128)(2,1)}, u32[]{:S(2)}) copy-start(bf16[1606,1536]{1,0:T(8,128)(2,1)} %concatenate.39) | copy-start | bytes 14800900
  227.5 38.7 %collective-permute-start.12 = (bf16[768,384]{1,0:T(8,128)(2,1)S(1)}, bf16[768,384]{1,0:T(8,128)(2,1)S(1)}, u32[]{:S(2)}, u32[]{:S(2)}) collective-permute-start(bf16[768,384]{1,0:T(8,128)(2,1)S(1)} %collective-permute-done.10), channel_id=1, source_target_pairs={{0,2},{2,4},{4,6},{6,8},{8,10},{10,12},{12,14},{14,0},{1,3},{3,5},... | collective-permute-start | bytes 1769480 | tf_op jit(solution)/shard_map/ppermute | solution.py:27
Sparse Core Ops, SparseCore 0:
  15.7 147.3 all-reduce.1
  271.5 6.8 reduce-scatter.1
